TPU v7x, 32 devices: a whole 2x2x4 slice. The times are simulated.
32 devices in a mesh: dp: 8 (over z, y), mp: 4 (over x, core).
Axes of the slice: x: 2, y: 2, z: 4, core: 2. Of those that a mesh axis runs over, the one named last changes fastest.
Arguments:
- patches: bfloat16 [32, 256, 768], P('dp'), may hold values from -20 to 20
- segment_ids: int32 [32, 256], P('dp'), may hold values from 0 to 1, never falling along the last dimension, each value on 1 to 196 neighbouring positions
- mask_slots: int32 [32, 64], P('dp'), may hold values from 0 to 255
- gain_attn: bfloat16 [768], replicated, may hold values from 0.099609375 to 1.8984375
- qkv_weight: bfloat16 [3, 768, 768], P(None, None, 'mp'), may hold values from -0.21875 to 0.21875
- out_weight: bfloat16 [768, 768], P('mp'), may hold values from -2 to 2
- gain_mlp: bfloat16 [768], replicated, may hold values from 0.099609375 to 1.8984375
- up_weight: bfloat16 [768, 3072], P(None, 'mp'), may hold values from -0.21875 to 0.21875
- down_weight: bfloat16 [3072, 768], P('mp'), may hold values from -0.109375 to 0.109375
- embed_weight: bfloat16 [768, 384], P(None, 'mp'), may hold values from -0.21875 to 0.21875
- mask_token: bfloat16 [384], replicated, may hold values from -4 to 4
- pred_gain_attn: bfloat16 [384], replicated, may hold values from 0.099609375 to 1.8984375
- pred_qkv: bfloat16 [3, 384, 384], P(None, None, 'mp'), may hold values from -0.3125 to 0.3125
- pred_out: bfloat16 [384, 384], P('mp'), may hold values from -3 to 3
- pred_gain_mlp: bfloat16 [384], replicated, may hold values from 0.099609375 to 1.8984375
- pred_up: bfloat16 [384, 1536], P(None, 'mp'), may hold values from -0.3125 to 0.3125
- pred_down: bfloat16 [1536, 384], P('mp'), may hold values from -0.15625 to 0.15625
- cotangent: bfloat16 [32, 256, 384], P('dp'), may hold values from -6 to 6
Outputs:
- predictions: bfloat16 [32, 256, 384], P('dp')
- patches_grad: bfloat16 [32, 256, 768], P('dp')
- variance: float32 [384], P('mp')
- grad_gain_attn: float32 [768], P('dp')
- grad_qkv: float32 [3, 768, 768], P(None, 'dp', 'mp')
- grad_out: float32 [768, 768], P('mp', 'dp')
- grad_gain_mlp: float32 [768], P('dp')
- grad_up: float32 [768, 3072], P('dp', 'mp')
- grad_down: float32 [3072, 768], P('mp', 'dp')
- grad_embed: float32 [768, 384], P('dp', 'mp')
- grad_mask_token: float32 [384], P('dp')
- grad_pred_gain_attn: float32 [384], P('dp')
- grad_pred_qkv: float32 [3, 384, 384], P(None, 'dp', 'mp')
- grad_pred_out: float32 [384, 384], P('mp', 'dp')
- grad_pred_gain_mlp: float32 [384], P('dp')
- grad_pred_up: float32 [384, 1536], P('dp', 'mp')
- grad_pred_down: float32 [1536, 384], P('mp', 'dp')
Inputs may be any that keep to these rules, and one draw needn't show every extreme that they name: `segment_ids`: each row holds image 0 then image 1, each of 60 to 196 tokens. `mask_slots`: positions within the row that take the mask token; a position may repeat.
All inputs are finite; a program needn't handle non-finite values.
Results may differ from a plain program's by a relative error of at most 0.03.
Values may be sent and summed in bfloat16 or wider, within the bound.
No kernel may reach another device: no remote copies, remote signals or barrier semaphores. Data moves between devices by JAX's collectives and lax.ppermute only.
A program may use at most 128 MiB of HBM per device.

v0:
```python
from functools import partial

import jax
import jax.numpy as jnp
from jax import lax
from jax.sharding import PartitionSpec as P

HEAD_DIM = 64
P_HEAD_DIM = 32


EPS = 1e-06


def norm_rows(value, gain):
    mean = jnp.mean(value, -1, keepdims=True)
    centred = value - mean
    spread = jnp.mean(centred * centred, -1, keepdims=True)
    return centred * lax.rsqrt(spread + EPS) * gain


def across_heads(portion):
    share = lax.psum_scatter(portion, "mp", scatter_dimension=0, tiled=True)
    return lax.all_gather(share, "mp", axis=0, tiled=True)


def unchanged(portion):
    return portion


def heads_of(matrix, seqs, head_dim):
    return matrix.reshape(seqs, -1, matrix.shape[1] // head_dim, head_dim)


def scores_of(query_h, keys_h, same, head_dim):
    scores = jnp.einsum(
        "sqhd,skhd->shqk", query_h, keys_h, preferred_element_type=jnp.float32
    ) * head_dim ** (-0.5)
    return jnp.where(same[:, None], scores, -1000000000.0)


def block_forward(value, weights, same, head_dim, combine, spread):
    gain_one, w_qkv, w_out, gain_two, w_up, w_down = weights
    seqs = same.shape[0]
    normed = spread(norm_rows(value, gain_one).astype(jnp.bfloat16))
    query = jnp.dot(normed, w_qkv[0], preferred_element_type=jnp.float32).astype(jnp.bfloat16)
    keys = jnp.dot(normed, w_qkv[1], preferred_element_type=jnp.float32).astype(jnp.bfloat16)
    values = jnp.dot(normed, w_qkv[2], preferred_element_type=jnp.float32).astype(jnp.bfloat16)
    scores = scores_of(
        heads_of(query, seqs, head_dim), heads_of(keys, seqs, head_dim), same, head_dim
    )
    top = jnp.max(scores, -1, keepdims=True)
    expd = jnp.exp(scores - top)
    total = jnp.sum(expd, -1, keepdims=True)
    probs_low = (expd / total).astype(jnp.bfloat16)
    logsum = top + jnp.log(total)
    mixed = jnp.einsum(
        "shqk,skhd->sqhd",
        probs_low,
        heads_of(values, seqs, head_dim),
        preferred_element_type=jnp.float32,
    )
    mixed = mixed.reshape(query.shape).astype(jnp.bfloat16)
    middle = value + combine(jnp.dot(mixed, w_out, preferred_element_type=jnp.float32))
    second = spread(norm_rows(middle, gain_two).astype(jnp.bfloat16))
    before = jnp.dot(second, w_up, preferred_element_type=jnp.float32)
    hidden = jax.nn.gelu(before, approximate=False).astype(jnp.bfloat16)
    output = middle + combine(jnp.dot(hidden, w_down, preferred_element_type=jnp.float32))
    return (
        output,
        (value, normed, query, keys, values, logsum, mixed, middle, second, before, hidden),
    )


def block_backward(grad, kept, weights, same, head_dim, combine, spread):
    gain_one, w_qkv, w_out, gain_two, w_up, w_down = weights
    value, normed, query, keys, values, logsum, mixed, middle, second, before, hidden = kept
    seqs = same.shape[0]
    grad_low = spread(grad.astype(jnp.bfloat16))
    d_down = jnp.dot(hidden.T, grad_low, preferred_element_type=jnp.float32)
    d_hidden = jnp.dot(grad_low, w_down.T, preferred_element_type=jnp.float32)
    gelu_back = jax.vjp(partial(jax.nn.gelu, approximate=False), before)[1]
    d_before = gelu_back(d_hidden)[0].astype(jnp.bfloat16)
    d_up = jnp.dot(second.T, d_before, preferred_element_type=jnp.float32)
    d_second = combine(jnp.dot(d_before, w_up.T, preferred_element_type=jnp.float32))
    second_back = jax.vjp(norm_rows, middle, gain_two)[1]
    d_middle, d_gain_two = second_back(d_second)
    grad_mid = grad + d_middle
    mid_low = spread(grad_mid.astype(jnp.bfloat16))
    d_out = jnp.dot(mixed.T, mid_low, preferred_element_type=jnp.float32)
    d_mixed = jnp.dot(mid_low, w_out.T, preferred_element_type=jnp.float32).astype(jnp.bfloat16)
    query_h = heads_of(query, seqs, head_dim)
    keys_h = heads_of(keys, seqs, head_dim)
    values_h = heads_of(values, seqs, head_dim)
    mixed_h = heads_of(d_mixed, seqs, head_dim)
    probs = jnp.exp(scores_of(query_h, keys_h, same, head_dim) - logsum)
    d_probs = jnp.einsum("sqhd,skhd->shqk", mixed_h, values_h, preferred_element_type=jnp.float32)
    d_scores = (probs * (d_probs - jnp.sum(d_probs * probs, -1, keepdims=True))).astype(
        jnp.bfloat16
    )
    scale = head_dim ** (-0.5)
    d_query = (
        (
            jnp.einsum("shqk,skhd->sqhd", d_scores, keys_h, preferred_element_type=jnp.float32)
            * scale
        )
        .reshape(query.shape)
        .astype(jnp.bfloat16)
    )
    d_keys = (
        (
            jnp.einsum("shqk,sqhd->skhd", d_scores, query_h, preferred_element_type=jnp.float32)
            * scale
        )
        .reshape(query.shape)
        .astype(jnp.bfloat16)
    )
    d_values = (
        jnp.einsum(
            "shqk,sqhd->skhd",
            probs.astype(jnp.bfloat16),
            mixed_h,
            preferred_element_type=jnp.float32,
        )
        .reshape(query.shape)
        .astype(jnp.bfloat16)
    )
    d_qkv = jnp.stack(
        [
            jnp.dot(normed.T, d_query, preferred_element_type=jnp.float32),
            jnp.dot(normed.T, d_keys, preferred_element_type=jnp.float32),
            jnp.dot(normed.T, d_values, preferred_element_type=jnp.float32),
        ]
    )
    d_normed = (
        jnp.dot(d_query, w_qkv[0].T, preferred_element_type=jnp.float32)
        + jnp.dot(d_keys, w_qkv[1].T, preferred_element_type=jnp.float32)
        + jnp.dot(d_values, w_qkv[2].T, preferred_element_type=jnp.float32)
    )
    d_normed = combine(d_normed)
    first_back = jax.vjp(norm_rows, value, gain_one)[1]
    d_value, d_gain_one = first_back(d_normed)
    return (grad_mid + d_value, (d_gain_one, d_qkv, d_out, d_gain_two, d_up, d_down))


def body(
    patches,
    segment_ids,
    mask_slots,
    gain_attn,
    qkv_weight,
    out_weight,
    gain_mlp,
    up_weight,
    down_weight,
    embed_weight,
    mask_token,
    pred_gain_attn,
    pred_qkv,
    pred_out,
    pred_gain_mlp,
    pred_up,
    pred_down,
    cotangent,
):
    seqs, length, width = patches.shape
    channels = cotangent.shape[2]
    model_size = lax.axis_size("mp")
    model_index = lax.axis_index("mp")
    portion_cols = channels // model_size
    token_rows = patches.shape[0] * length
    same = segment_ids[:, :, None] == segment_ids[:, None, :]
    positions = jnp.arange(length, dtype=jnp.int32)
    masked = jnp.any(positions[None, :, None] == mask_slots[:, None, :], -1).reshape(token_rows, 1)
    flat_input = patches.reshape(token_rows, width)
    flat_grad = cotangent.reshape(token_rows, channels)
    enc_weights = (
        gain_attn.astype(jnp.float32),
        qkv_weight,
        out_weight,
        gain_mlp.astype(jnp.float32),
        up_weight,
        down_weight,
    )
    pred_weights = (
        pred_gain_attn.astype(jnp.float32),
        pred_qkv,
        pred_out,
        pred_gain_mlp.astype(jnp.float32),
        pred_up,
        pred_down,
    )
    encoded, enc_kept = block_forward(
        flat_input.astype(jnp.float32), enc_weights, same, HEAD_DIM, across_heads, unchanged
    )
    enc_low = unchanged(encoded.astype(jnp.bfloat16))
    embed_part = jnp.dot(enc_low, embed_weight, preferred_element_type=jnp.float32)
    embedded = lax.all_gather(embed_part, "mp", axis=1, tiled=True)
    start_pred = jnp.where(masked, mask_token.astype(jnp.float32), embedded)
    predicted, pred_kept = block_forward(
        start_pred, pred_weights, same, P_HEAD_DIM, across_heads, unchanged
    )
    grad_start, pred_grads = block_backward(
        flat_grad.astype(jnp.float32),
        pred_kept,
        pred_weights,
        same,
        P_HEAD_DIM,
        across_heads,
        unchanged,
    )
    d_token = jnp.sum(jnp.where(masked, grad_start, 0.0), 0)
    d_embedded = jnp.where(masked, 0.0, grad_start).astype(jnp.bfloat16)
    d_local = lax.dynamic_slice_in_dim(d_embedded, model_index * portion_cols, portion_cols, 1)
    d_embed = jnp.dot(enc_low.T, d_local, preferred_element_type=jnp.float32)
    grad_enc = across_heads(jnp.dot(d_local, embed_weight.T, preferred_element_type=jnp.float32))
    grad_input, enc_grads = block_backward(
        grad_enc, enc_kept, enc_weights, same, HEAD_DIM, across_heads, unchanged
    )
    d_gain_one, d_qkv, d_out, d_gain_two, d_up, d_down = enc_grads
    p_gain_one, p_qkv, p_out, p_gain_two, p_up, p_down = pred_grads
    channel = lax.dynamic_slice_in_dim(predicted, model_index * portion_cols, portion_cols, 1)
    local_first = jnp.sum(channel, 0)
    local_squares = jnp.sum(channel * channel, 0)
    pred_low = predicted.astype(jnp.bfloat16)
    input_low = grad_input.astype(jnp.bfloat16)
    stat_sums = lax.psum((local_first, local_squares), "dp")
    token_count = seqs * length * lax.axis_size("dp")
    channel_mean = stat_sums[0] / token_count
    variance = stat_sums[1] / token_count - channel_mean * channel_mean
    reduced = (
        lax.psum_scatter(d_gain_one, "dp", scatter_dimension=0, tiled=True),
        lax.psum_scatter(d_qkv, "dp", scatter_dimension=1, tiled=True),
        lax.psum_scatter(d_out, "dp", scatter_dimension=1, tiled=True),
        lax.psum_scatter(d_gain_two, "dp", scatter_dimension=0, tiled=True),
        lax.psum_scatter(d_up, "dp", scatter_dimension=0, tiled=True),
        lax.psum_scatter(d_down, "dp", scatter_dimension=1, tiled=True),
        lax.psum_scatter(d_embed, "dp", scatter_dimension=0, tiled=True),
        lax.psum_scatter(d_token, "dp", scatter_dimension=0, tiled=True),
        lax.psum_scatter(p_gain_one, "dp", scatter_dimension=0, tiled=True),
        lax.psum_scatter(p_qkv, "dp", scatter_dimension=1, tiled=True),
        lax.psum_scatter(p_out, "dp", scatter_dimension=1, tiled=True),
        lax.psum_scatter(p_gain_two, "dp", scatter_dimension=0, tiled=True),
        lax.psum_scatter(p_up, "dp", scatter_dimension=0, tiled=True),
        lax.psum_scatter(p_down, "dp", scatter_dimension=1, tiled=True),
    )
    predictions = pred_low.reshape(seqs, length, channels)
    patches_grad = input_low.reshape(seqs, length, width)
    return (
        predictions,
        patches_grad,
        variance,
        reduced[0],
        reduced[1],
        reduced[2],
        reduced[3],
        reduced[4],
        reduced[5],
        reduced[6],
        reduced[7],
        reduced[8],
        reduced[9],
        reduced[10],
        reduced[11],
        reduced[12],
        reduced[13],
    )


def solution(mesh):
    placed = (
        P("dp", None, None),
        P("dp", None),
        P("dp", None),
        P(),
        P(None, None, "mp"),
        P("mp", None),
        P(),
        P(None, "mp"),
        P("mp", None),
        P(None, "mp"),
        P(),
        P(),
        P(None, None, "mp"),
        P("mp", None),
        P(),
        P(None, "mp"),
        P("mp", None),
        P("dp", None, None),
    )
    return jax.shard_map(
        body,
        mesh=mesh,
        in_specs=placed,
        out_specs=(
            P("dp", None, None),
            P("dp", None, None),
            P("mp"),
            P("dp"),
            P(None, "dp", "mp"),
            P("mp", "dp"),
            P("dp"),
            P("dp", "mp"),
            P("mp", "dp"),
            P("dp", "mp"),
            P("dp"),
            P("dp"),
            P(None, "dp", "mp"),
            P("mp", "dp"),
            P("dp"),
            P("dp", "mp"),
            P("mp", "dp"),
        ),
        check_vma=False,
    )
```

profile of v0, /device:TPU:0, one launch (start us, length us, event | category | flops | bytes accessed | tf_op | source)
XLA Modules:
  0.0 1332.0 jit_solution(11685086918363662859)
XLA Ops:
  28.6 40.8 %reduce-scatter.22.cloned.1.call-done = f32[256,768]{1,0:T(8,128)} async-done(((f32[1024,768]{1,0:T(8,128)}), f32[256,768]{1,0:T(8,128)}) %reduce-scatter.22.cloned.1.call-update) | async-done | bytes 786448 | tf_op jit(solution)/shard_map/reduce_scatter | solution.py:23
  69.5 30.1 %all-gather.11.cloned.1.call-done = f32[1024,768]{1,0:T(8,128)} async-done(((f32[256,768]{1,0:T(8,128)}), f32[1024,768]{1,0:T(8,128)}) %all-gather.11.cloned.1.call-update) | async-done | bytes 3145744 | tf_op jit(solution)/shard_map/all_gather | solution.py:24
  103.5 9.5 multiply_convert_fusion.2
  117.3 38.1 %reduce-scatter.24.cloned.1.call-done = f32[256,768]{1,0:T(8,128)} async-done(((f32[1024,768]{1,0:T(8,128)}), f32[256,768]{1,0:T(8,128)}) %reduce-scatter.24.cloned.1.call-update) | async-done | bytes 786448 | tf_op jit(solution)/shard_map/reduce_scatter | solution.py:23
  155.4 29.9 %all-gather.13.cloned.1.call-done = f32[1024,768]{1,0:T(8,128)} async-done(((f32[256,768]{1,0:T(8,128)}), f32[1024,768]{1,0:T(8,128)}) %all-gather.13.cloned.1.call-update) | async-done | bytes 3145744 | tf_op jit(solution)/shard_map/all_gather | solution.py:24
  191.7 19.1 %all-gather.15.cloned.1.call-done = f32[1024,384]{0,1:T(8,128)} async-done(((f32[1024,96]{0,1:T(8,128)}), f32[1024,384]{0,1:T(8,128)}) %all-gather.15.cloned.1.call-update) | async-done | bytes 1572880 | tf_op jit(solution)/shard_map/all_gather | solution.py:198
  229.3 28.3 %reduce-scatter.26.cloned.1.call-done = f32[256,384]{0,1:T(8,128)} async-done(((f32[1024,384]{0,1:T(8,128)}), f32[256,384]{0,1:T(8,128)}) %reduce-scatter.26.cloned.1.call-update) | async-done | bytes 393232 | tf_op jit(solution)/shard_map/reduce_scatter | solution.py:23
  257.7 21.2 %all-gather.17.cloned.1.call-done = f32[1024,384]{0,1:T(8,128)} async-done(((f32[256,384]{0,1:T(8,128)}), f32[1024,384]{0,1:T(8,128)}) %all-gather.17.cloned.1.call-update) | async-done | bytes 1572880 | tf_op jit(solution)/shard_map/all_gather | solution.py:24
  296.2 23.2 %reduce-scatter.30.cloned.1.call-done = f32[256,384]{0,1:T(8,128)} async-done(((f32[1024,384]{0,1:T(8,128)}), f32[256,384]{0,1:T(8,128)}) %reduce-scatter.30.cloned.1.call-update) | async-done | bytes 393232 | tf_op jit(solution)/shard_map/reduce_scatter | solution.py:23
  319.5 31.2 %reduce-scatter.28.cloned.1.call-done = f32[256,384]{0,1:T(8,128)} async-done(((f32[1024,384]{0,1:T(8,128)}), f32[256,384]{0,1:T(8,128)}) %reduce-scatter.28.cloned.1.call-update) | async-done | bytes 393232 | tf_op jit(solution)/shard_map/reduce_scatter | solution.py:23
  354.0 17.9 %all-gather.21.cloned.1.call-done = f32[1024,384]{0,1:T(8,128)} async-done(((f32[256,384]{0,1:T(8,128)}), f32[1024,384]{0,1:T(8,128)}) %all-gather.21.cloned.1.call-update) | async-done | bytes 1572880 | tf_op jit(solution)/shard_map/all_gather | solution.py:24
  375.5 17.8 %all-gather.19.cloned.1.call-done = f32[1024,384]{0,1:T(8,128)} async-done(((f32[256,384]{0,1:T(8,128)}), f32[1024,384]{0,1:T(8,128)}) %all-gather.19.cloned.1.call-update) | async-done | bytes 1572880 | tf_op jit(solution)/shard_map/all_gather | solution.py:24
  411.8 28.2 %reduce-scatter.32.cloned.1.call-done = f32[256,384]{0,1:T(8,128)} async-done(((f32[1024,384]{0,1:T(8,128)}), f32[256,384]{0,1:T(8,128)}) %reduce-scatter.32.cloned.1.call-update) | async-done | bytes 393232 | tf_op jit(solution)/shard_map/reduce_scatter | solution.py:23
  440.1 21.2 %all-gather.23.cloned.1.call-done = f32[1024,384]{0,1:T(8,128)} async-done(((f32[256,384]{0,1:T(8,128)}), f32[1024,384]{0,1:T(8,128)}) %all-gather.23.cloned.1.call-update) | async-done | bytes 1572880 | tf_op jit(solution)/shard_map/all_gather | solution.py:24
  470.6 38.0 %reduce-scatter.34.cloned.1.call-done = f32[256,768]{1,0:T(8,128)} async-done(((f32[1024,768]{1,0:T(8,128)}), f32[256,768]{1,0:T(8,128)}) %reduce-scatter.34.cloned.1.call-update) | async-done | bytes 786448 | tf_op jit(solution)/shard_map/reduce_scatter | solution.py:23
  508.7 30.0 %all-gather.25.cloned.1.call-done = f32[1024,768]{1,0:T(8,128)} async-done(((f32[256,768]{1,0:T(8,128)}), f32[1024,768]{1,0:T(8,128)}) %all-gather.25.cloned.1.call-update) | async-done | bytes 3145744 | tf_op jit(solution)/shard_map/all_gather | solution.py:24
  538.7 6.2 add_convert_fusion.1
  549.3 38.1 %reduce-scatter.36.cloned.1.call-done = f32[256,768]{1,0:T(8,128)} async-done(((f32[1024,768]{1,0:T(8,128)}), f32[256,768]{1,0:T(8,128)}) %reduce-scatter.36.cloned.1.call-update) | async-done | bytes 786448 | tf_op jit(solution)/shard_map/reduce_scatter | solution.py:23
  588.5 28.9 %all-gather.27.cloned.1.call-done = f32[1024,768]{1,0:T(8,128)} async-done(((f32[256,768]{1,0:T(8,128)}), f32[1024,768]{1,0:T(8,128)}) %all-gather.27.cloned.1.call-update) | async-done | bytes 3145744 | tf_op jit(solution)/shard_map/all_gather | solution.py:24
  665.4 13.9 %reduce-scatter.38.cloned.1.call-done = f32[256,768]{1,0:T(8,128)} async-done(((f32[1024,768]{1,0:T(8,128)}), f32[256,768]{1,0:T(8,128)}) %reduce-scatter.38.cloned.1.call-update) | async-done | bytes 786448 | tf_op jit(solution)/shard_map/reduce_scatter | solution.py:23
  696.4 5.4 fusion.134
  706.7 51.2 %all-reduce.9.cloned.1.call-done = f32[3,384,96]{2,0,1:T(4,128)} async-done(((f32[3,384,96]{2,0,1:T(4,128)}), f32[3,384,96]{2,0,1:T(4,128)}) %all-reduce.9.cloned.1.call-update) | async-done | bytes 442384
  759.4 63.3 %reduce-scatter.54.cloned.1.call-done = f32[96,192]{1,0:T(8,128)} async-done(((f32[768,192]{1,0:T(8,128)}), f32[96,192]{1,0:T(8,128)}) %reduce-scatter.54.cloned.1.call-update) | async-done | bytes 73744
  824.3 67.8 %reduce-scatter.52.cloned.1.call-done = f32[96,576]{1,0:T(8,128)} async-done(((f32[768,576]{1,0:T(8,128)}), f32[96,576]{1,0:T(8,128)}) %reduce-scatter.52.cloned.1.call-update) | async-done | bytes 221200
  894.1 27.2 %all-gather.29.cloned.1.call-done = f32[1024,768]{1,0:T(8,128)} async-done(((f32[256,768]{1,0:T(8,128)}), f32[1024,768]{1,0:T(8,128)}) %all-gather.29.cloned.1.call-update) | async-done | bytes 3145744 | tf_op jit(solution)/shard_map/all_gather | solution.py:24
  925.8 37.4 %all-reduce.6 = (f32[96]{0:T(128)S(1)}, f32[96]{0:T(128)S(1)}, f32[768]{0:T(1024)S(1)}, f32[768]{0:T(1024)S(1)}, f32[384]{0:T(512)S(1)}, /*index=5*/f32[384]{0:T(512)S(1)}, f32[384]{0:T(512)S(1)}) all-reduce(f32[96]{0:T(128)S(1)} %get-tuple-element.94, f32[96]{0:T(128)S(1)} %get-tuple-element.93, ...), channel_id=1, replica_groups=mesh['dp'=8,'mp'=4] {'dp'}, use_global_device_ids=true, to_apply=%region_35.36 | all-reduce | flops 2880 | bytes 23040 | tf_op jit(solution)/shard_map/psum | solution.py:227
  971.0 16.2 %reduce-scatter.50.cloned.1.call-done = f32[384,48]{0,1:T(8,128)} async-done(((f32[384,384]{0,1:T(8,128)}), f32[384,48]{0,1:T(8,128)}) %reduce-scatter.50.cloned.1.call-update) | async-done | bytes 73744 | tf_op jit(solution)/shard_map/reduce_scatter | solution.py:245
  987.3 65.3 %reduce-scatter.48.cloned.1.call-done = f32[48,384]{1,0:T(8,128)} async-done(((f32[384,384]{1,0:T(8,128)}), f32[48,384]{1,0:T(8,128)}) %reduce-scatter.48.cloned.1.call-update) | async-done | bytes 73744 | tf_op jit(solution)/shard_map/reduce_scatter | solution.py:244
  1052.5 63.9 %reduce-scatter.46.cloned.1.call-done = f32[96,48]{0,1:T(8,128)} async-done(((f32[96,384]{0,1:T(8,128)}), f32[96,48]{0,1:T(8,128)}) %reduce-scatter.46.cloned.1.call-update) | async-done | bytes 18448 | tf_op jit(solution)/shard_map/reduce_scatter | solution.py:242
  1116.5 64.2 %reduce-scatter.44.cloned.1.call-done = f32[96,96]{1,0:T(8,128)} async-done(((f32[768,96]{1,0:T(8,128)}), f32[96,96]{1,0:T(8,128)}) %reduce-scatter.44.cloned.1.call-update) | async-done | bytes 36880 | tf_op jit(solution)/shard_map/reduce_scatter | solution.py:238
  1180.6 72.0 %reduce-scatter.42.cloned.1.call-done = f32[768,96]{0,1:T(8,128)} async-done(((f32[768,768]{0,1:T(8,128)}), f32[768,96]{0,1:T(8,128)}) %reduce-scatter.42.cloned.1.call-update) | async-done | bytes 294928 | tf_op jit(solution)/shard_map/reduce_scatter | solution.py:237
  1252.6 72.1 %reduce-scatter.40.cloned.1.call-done = f32[96,768]{1,0:T(8,128)} async-done(((f32[768,768]{1,0:T(8,128)}), f32[96,768]{1,0:T(8,128)}) %reduce-scatter.40.cloned.1.call-update) | async-done | bytes 294928 | tf_op jit(solution)/shard_map/reduce_scatter | solution.py:236
  (456 shorter events, 196.6 us)
Async XLA Ops:
  7.2 96.3 %copy-start = (bf16[768,768]{1,0:T(8,128)(2,1)S(1)}, bf16[768,768]{1,0:T(8,128)(2,1)}, u32[]{:S(2)}) copy-start(bf16[768,768]{1,0:T(8,128)(2,1)} %param.25) | copy-start | bytes 3538948
  7.2 62.2 %reduce-scatter.22.cloned.1.call-start = ((), (), s32[]{:S(2)}) async-start(), calls=%async_computation.17 | async-start | bytes 3932160 | tf_op jit(solution)/shard_map/reduce_scatter | solution.py:23
  28.6 71.0 %all-gather.11.cloned.1.call-start = ((), (), s32[]{:S(2)}) async-start(), calls=%async_computation.18 | async-start | bytes 3932160 | tf_op jit(solution)/shard_map/all_gather | solution.py:24
  69.4 85.9 %reduce-scatter.24.cloned.1.call-start = ((), (), s32[]{:S(2)}) async-start(), calls=%async_computation.19 | async-start | bytes 3932160 | tf_op jit(solution)/shard_map/reduce_scatter | solution.py:23
  117.2 68.1 %all-gather.13.cloned.1.call-start = ((), (), s32[]{:S(2)}) async-start(), calls=%async_computation.20 | async-start | bytes 3932160 | tf_op jit(solution)/shard_map/all_gather | solution.py:24
  155.4 55.4 %all-gather.15.cloned.1.call-start = ((), (), s32[]{:S(2)}) async-start(), calls=%async_computation.21 | async-start | bytes 1966080 | tf_op jit(solution)/shard_map/all_gather | solution.py:198
  191.0 66.6 %reduce-scatter.26.cloned.1.call-start = ((), (), s32[]{:S(2)}) async-start(), calls=%async_computation.22 | async-start | bytes 1966080 | tf_op jit(solution)/shard_map/reduce_scatter | solution.py:23
  191.7 87.3 %copy-start.80 = (pred[1024]{0:T(1024)(128)(4,1)}, pred[1024]{0:T(1024)(128)(4,1)S(1)}, u32[]{:S(2)}) copy-start(pred[1024]{0:T(1024)(128)(4,1)S(1)} %broadcast_in_dim.70) | copy-start | bytes 3076
  191.7 87.2 %copy-start.74 = (f32[384]{0:T(512)}, f32[384]{0:T(512)S(1)}, u32[]{:S(2)}) copy-start(f32[384]{0:T(512)S(1)} %convert_element_type.211) | copy-start | bytes 4612
  229.3 49.7 %all-gather.17.cloned.1.call-start = ((), (), s32[]{:S(2)}) async-start(), calls=%async_computation.23 | async-start | bytes 1966080 | tf_op jit(solution)/shard_map/all_gather | solution.py:24
  257.6 61.8 %reduce-scatter.30.cloned.1.call-start = ((), (), s32[]{:S(2)}) async-start(), calls=%async_computation.26 | async-start | bytes 1966080 | tf_op jit(solution)/shard_map/reduce_scatter | solution.py:23
  291.1 59.6 %reduce-scatter.28.cloned.1.call-start = ((), (), s32[]{:S(2)}) async-start(), calls=%async_computation.24 | async-start | bytes 1966080 | tf_op jit(solution)/shard_map/reduce_scatter | solution.py:23
  296.2 75.7 %all-gather.21.cloned.1.call-start = ((), (), s32[]{:S(2)}) async-start(), calls=%async_computation.27 | async-start | bytes 1966080 | tf_op jit(solution)/shard_map/all_gather | solution.py:24
  319.5 73.8 %all-gather.19.cloned.1.call-start = ((), (), s32[]{:S(2)}) async-start(), calls=%async_computation.25 | async-start | bytes 1966080 | tf_op jit(solution)/shard_map/all_gather | solution.py:24
  350.8 89.3 %reduce-scatter.32.cloned.1.call-start = ((), (), s32[]{:S(2)}) async-start(), calls=%async_computation.28 | async-start | bytes 1966080 | tf_op jit(solution)/shard_map/reduce_scatter | solution.py:23
  411.8 49.6 %all-gather.23.cloned.1.call-start = ((), (), s32[]{:S(2)}) async-start(), calls=%async_computation.29 | async-start | bytes 1966080 | tf_op jit(solution)/shard_map/all_gather | solution.py:24
  440.1 68.6 %reduce-scatter.34.cloned.1.call-start = ((), (), s32[]{:S(2)}) async-start(), calls=%async_computation.30 | async-start | bytes 3932160 | tf_op jit(solution)/shard_map/reduce_scatter | solution.py:23
  470.6 68.1 %all-gather.25.cloned.1.call-start = ((), (), s32[]{:S(2)}) async-start(), calls=%async_computation.31 | async-start | bytes 3932160 | tf_op jit(solution)/shard_map/all_gather | solution.py:24
  508.7 78.7 %reduce-scatter.36.cloned.1.call-start = ((), (), s32[]{:S(2)}) async-start(), calls=%async_computation.32 | async-start | bytes 3932160 | tf_op jit(solution)/shard_map/reduce_scatter | solution.py:23
  549.3 68.1 %all-gather.27.cloned.1.call-start = ((), (), s32[]{:S(2)}) async-start(), calls=%async_computation.33 | async-start | bytes 3932160 | tf_op jit(solution)/shard_map/all_gather | solution.py:24
  587.4 91.9 %reduce-scatter.38.cloned.1.call-start = ((), (), s32[]{:S(2)}) async-start(), calls=%async_computation.34 | async-start | bytes 3932160 | tf_op jit(solution)/shard_map/reduce_scatter | solution.py:23
  641.2 116.7 %all-reduce.9.cloned.1.call-start = ((), (), s32[]{:S(2)}) async-start(), calls=%async_computation.44 | async-start | bytes 1572864
  647.3 175.4 %reduce-scatter.54.cloned.1.call-start = ((), (), s32[]{:S(2)}) async-start(), calls=%async_computation.43 | async-start | bytes 884736
  651.2 241.0 %reduce-scatter.52.cloned.1.call-start = ((), (), s32[]{:S(2)}) async-start(), calls=%async_computation.42 | async-start | bytes 2211840
  665.4 255.9 %all-gather.29.cloned.1.call-start = ((), (), s32[]{:S(2)}) async-start(), calls=%async_computation.35 | async-start | bytes 3932160 | tf_op jit(solution)/shard_map/all_gather | solution.py:24
  679.4 307.9 %reduce-scatter.50.cloned.1.call-start = ((), (), s32[]{:S(2)}) async-start(), calls=%async_computation.41 | async-start | bytes 663552 | tf_op jit(solution)/shard_map/reduce_scatter | solution.py:245
  682.1 370.5 %reduce-scatter.48.cloned.1.call-start = ((), (), s32[]{:S(2)}) async-start(), calls=%async_computation.40 | async-start | bytes 663552 | tf_op jit(solution)/shard_map/reduce_scatter | solution.py:244
  685.3 431.2 %reduce-scatter.46.cloned.1.call-start = ((), (), s32[]{:S(2)}) async-start(), calls=%async_computation.39 | async-start | bytes 221184 | tf_op jit(solution)/shard_map/reduce_scatter | solution.py:242
  687.4 493.3 %reduce-scatter.44.cloned.1.call-start = ((), (), s32[]{:S(2)}) async-start(), calls=%async_computation.38 | async-start | bytes 442368 | tf_op jit(solution)/shard_map/reduce_scatter | solution.py:238
  690.4 562.3 %reduce-scatter.42.cloned.1.call-start = ((), (), s32[]{:S(2)}) async-start(), calls=%async_computation.37 | async-start | bytes 2654208 | tf_op jit(solution)/shard_map/reduce_scatter | solution.py:237
  695.7 629.0 %reduce-scatter.40.cloned.1.call-start = ((), (), s32[]{:S(2)}) async-start(), calls=%async_computation.36 | async-start | bytes 2654208 | tf_op jit(solution)/shard_map/reduce_scatter | solution.py:236
  704.4 216.9 %copy-start.79 = (f32[768]{0:T(1024)S(1)}, f32[768]{0:T(1024)}, u32[]{:S(2)}) copy-start(f32[768]{0:T(1024)} %copy-done.78) | copy-start | bytes 9220
  (122 other events, 623.8 us)
Sparse Core Ops, SparseCore 0:
  28.7 40.6 reduce-scatter.21
  71.1 28.5 all-gather.10
  117.3 37.9 reduce-scatter.23
  156.7 28.5 all-gather.12
  191.1 19.6 all-gather.14
  229.4 28.1 reduce-scatter.25
  259.2 19.6 all-gather.16
  291.2 28.1 reduce-scatter.29
  322.5 28.1 reduce-scatter.27
  352.2 19.6 all-gather.20
  373.6 19.6 all-gather.18
  411.9 28.1 reduce-scatter.31
  441.6 19.6 all-gather.22
  470.7 37.9 reduce-scatter.33
  510.1 28.5 all-gather.24
  549.4 37.9 reduce-scatter.35
  588.8 28.5 all-gather.26
  641.3 37.9 reduce-scatter.37
  683.1 74.7 all-reduce.8
  761.0 61.6 reduce-scatter.53
  826.6 65.5 reduce-scatter.51
  893.8 27.4 all-gather.28
  925.1 62.0 reduce-scatter.49
  991.3 61.1 reduce-scatter.47
  1056.4 60.0 reduce-scatter.45
  1120.2 60.4 reduce-scatter.43
  1184.5 68.0 reduce-scatter.41
  1256.7 67.9 reduce-scatter.39
where the time goes:
time: 1340 us; the launch traced here: 1330 us
  waiting for transfers between devices  1060 us (79%)
  matrix products  97.9 us (7%)
  local copies, waits for them, and re-layouts  62.2 us (5%)
  other arithmetic  54.9 us (4%)
  blocking collectives  37.4 us (3%)
  between operations  17.7 us (1%)
    reduce_scatter x9, waiting for transfers between devices, across_heads(): share = lax.psum_scatter(portion, 'mp', scatter_dimension=0, tiled=True)  280 us
    all_gather x9, waiting for transfers between devices, across_heads(): return lax.all_gather(share, 'mp', axis=0, tiled=True)  224 us
    unnamed x31, waiting for transfers between devices  183 us
    reduce_scatter x1, waiting for transfers between devices, body(): lax.psum_scatter(d_up, 'dp', scatter_dimension=0, tiled=True)  72.1 us
    reduce_scatter x1, waiting for transfers between devices, body(): lax.psum_scatter(d_down, 'dp', scatter_dimension=1, tiled=True)  72 us
    reduce_scatter x1, waiting for transfers between devices, body(): lax.psum_scatter(p_up, 'dp', scatter_dimension=0, tiled=True)  65.3 us
    reduce_scatter x1, waiting for transfers between devices, body(): lax.psum_scatter(d_embed, 'dp', scatter_dimension=0, tiled=True)  64.2 us
    reduce_scatter x1, waiting for transfers between devices, body(): lax.psum_scatter(p_out, 'dp', scatter_dimension=1, tiled=True)  63.9 us
  transfers between devices with their start and end apart: 28, of which 28 were waited for; matrix products, arithmetic and copies ran while one was open for 6% of the time, Pallas kernels for 0%

commit v1 on v0

v1 whole, which is shorter than its diff:
```python
import jax
import jax.numpy as jnp
from jax import lax
from jax.sharding import PartitionSpec as P

HEAD_DIM = 64
P_HEAD_DIM = 32
EPS = 1e-06
BF = jnp.bfloat16
F32 = jnp.float32


def swap(value, axis, bit):
    size = lax.axis_size(axis)
    return lax.ppermute(value, axis, [(i, i ^ bit) for i in range(size)])


def pick(value, index, axis=0):
    return lax.dynamic_index_in_dim(value, index, axis, keepdims=False)


def mm(spec, left, right):
    return jnp.einsum(spec, left, right, preferred_element_type=F32)


def norm_parts(value):
    mean = jnp.mean(value, -1, keepdims=True)
    centred = value - mean
    inverse = lax.rsqrt(jnp.mean(centred * centred, -1, keepdims=True) + EPS)
    return centred * inverse, inverse


def norm_back(normed, inverse, gain, grad):
    scaled = grad * gain
    along = jnp.mean(scaled * normed, -1, keepdims=True)
    d_value = (scaled - jnp.mean(scaled, -1, keepdims=True) - normed * along) * inverse
    return d_value, jnp.sum(grad * normed, 0)


def gather_shards(own):
    across = swap(own, "mp", 2)
    return [own, swap(own, "mp", 1), across, swap(across, "mp", 1)]


def block_forward(value, gains, weights, same, head_dim):
    w_q, w_k, w_v, w_o, w_up, w_down = weights
    length = value.shape[0]
    n_one, r_one = norm_parts(value)
    a = (n_one * gains[0]).astype(BF)
    heads = w_q.shape[0] // head_dim
    q, k, u = (mm("td,hd->ht", a, w).astype(BF).reshape(heads, head_dim, length) for w in (w_q, w_k, w_v))
    s = mm("hdq,hdk->hqk", q, k) * head_dim ** (-0.5)
    s = jnp.where(same, s, -1e9)
    expd = jnp.exp(s - jnp.max(s, -1, keepdims=True))
    p = expd / jnp.sum(expd, -1, keepdims=True)
    pb = p.astype(BF)
    o = mm("hqk,hdk->hdq", pb, u).astype(BF).reshape(-1, length)
    middle = value + mm("ht,hd->td", o, w_o)
    n_two, r_two = norm_parts(middle)
    b = (n_two * gains[1]).astype(BF)
    pre = mm("td,hd->th", b, w_up)
    cdf = 0.5 * (1.0 + lax.erf(pre * 0.7071067811865476))
    hid = (pre * cdf).astype(BF)
    slope = cdf + pre * (0.3989422804014327 * jnp.exp(-0.5 * pre * pre))
    out = middle + mm("th,hd->td", hid, w_down)
    return out, (n_one, r_one, a, q, k, u, pb, o, n_two, r_two, b, hid, slope)


def block_backward(grad, kept, gains, weights, head_dim):
    w_q, w_k, w_v, w_o, w_up, w_down = weights
    n_one, r_one, a, q, k, u, pb, o, n_two, r_two, b, hid, slope = kept
    length = grad.shape[0]
    shards = 4
    grad_low = grad.astype(BF)
    d_hid = mm("td,hd->th", grad_low, w_down)
    d_pre = (d_hid * slope).astype(BF)

    def weight_grad(left, right):
        return mm("td,tsc->sdc", left, right.reshape(length, shards, -1)).astype(BF)

    def weight_grad_t(left, right):
        return mm("td,sct->sdc", left, right.reshape(shards, -1, length)).astype(BF)

    g_down = weight_grad(grad_low, hid)
    g_up = weight_grad(b, d_pre)
    d_b = mm("th,hd->td", d_pre, w_up)
    d_middle, d_gain_two = norm_back(n_two, r_two, gains[1], d_b)
    grad_mid = grad + d_middle
    mid_low = grad_mid.astype(BF)
    g_out = weight_grad_t(mid_low, o)
    d_o = mm("hd,td->ht", w_o, mid_low).astype(BF).reshape(q.shape)
    p = pb.astype(F32)
    d_p = mm("hdq,hdk->hqk", d_o, u)
    d_s = (p * (d_p - jnp.sum(d_p * p, -1, keepdims=True))).astype(BF)
    scale = head_dim ** (-0.5)
    d_q = (mm("hqk,hdk->hdq", d_s, k) * scale).astype(BF).reshape(-1, length)
    d_k = (mm("hqk,hdq->hdk", d_s, q) * scale).astype(BF).reshape(-1, length)
    d_u = mm("hqk,hdq->hdk", pb, d_o).astype(BF).reshape(-1, length)
    g_q, g_k, g_v = (weight_grad_t(a, d) for d in (d_q, d_k, d_u))
    d_a = mm("ht,hd->td", d_q, w_q) + mm("ht,hd->td", d_k, w_k) + mm("ht,hd->td", d_u, w_v)
    d_value, d_gain_one = norm_back(n_one, r_one, gains[0], d_a)
    g_attn = jnp.concatenate([g_q, g_k, g_v, g_out], -1)
    return grad_mid + d_value, (g_attn, g_up, g_down), (d_gain_one, d_gain_two)


def reduce_shards(grads):
    away = swap(jnp.stack([grads[1], grads[3]]), "mp", 1)
    pair = jnp.stack([grads[0], grads[2]]).astype(F32) + away.astype(F32)
    other = swap(pair[1].astype(BF), "mp", 2)
    total = (pair[0] + other.astype(F32)).astype(BF)
    size = lax.axis_size("dp")
    rows = total.shape[0] // size
    parts = lax.all_to_all(total, "dp", 0, 0, tiled=True).reshape(size, rows, -1)
    return jnp.sum(parts.astype(F32), 0)


def spread_rows(value, me):
    across = swap(value, "mp", 2)
    both = jnp.stack([value, across])
    other = swap(both, "mp", 1)
    rel = jnp.stack([both[0], other[0], both[1], other[1]])
    return rel[jnp.arange(4) ^ me]


def body(
    patches, segment_ids, mask_slots, gain_attn, qkv_weight, out_weight, gain_mlp, up_weight, down_weight,
    embed_weight, mask_token, pred_gain_attn, pred_qkv, pred_out, pred_gain_mlp, pred_up, pred_down, cotangent,
):
    me = lax.axis_index("mp")
    dp_size = lax.axis_size("dp")
    length, width = patches.shape[1:]
    channels = cotangent.shape[2]
    value = pick(patches, me).astype(F32)
    segments = pick(segment_ids, me)
    slots = pick(mask_slots, me)
    grad = pick(cotangent, me).astype(F32)
    same = (segments[:, None] == segments[None, :])[None]
    masked = jnp.any(jnp.arange(length, dtype=jnp.int32)[:, None] == slots[None, :], -1, keepdims=True)

    attn_own = jnp.concatenate([jnp.swapaxes(qkv_weight, 1, 2).reshape(-1, width), out_weight], 0)
    attn = gather_shards(attn_own)
    up = gather_shards(up_weight.T)
    down = gather_shards(down_weight)
    embed = gather_shards(embed_weight.T)
    p_attn_own = jnp.concatenate([jnp.swapaxes(pred_qkv, 1, 2).reshape(-1, channels), pred_out], 0)
    pred = gather_shards(jnp.concatenate([p_attn_own, pred_up.T, pred_down], 0))

    def attn_parts(packs, n):
        stacked = jnp.stack([p[: 4 * n].reshape(4, n, -1) for p in packs], 1)
        return tuple(stacked[i].reshape(4 * n, -1) for i in range(4))

    hd = qkv_weight.shape[2]
    p_hd = pred_qkv.shape[2]
    p_hid = pred_up.shape[1]
    enc_w = attn_parts(attn, hd) + (jnp.concatenate(up, 0), jnp.concatenate(down, 0))
    pred_w = attn_parts(pred, p_hd) + (
        jnp.concatenate([p[4 * p_hd : 4 * p_hd + p_hid] for p in pred], 0),
        jnp.concatenate([p[4 * p_hd + p_hid :] for p in pred], 0),
    )
    embed_all = jnp.stack(embed)[jnp.arange(4) ^ me].reshape(channels, width)
    enc_gains = (gain_attn.astype(F32), gain_mlp.astype(F32))
    pred_gains = (pred_gain_attn.astype(F32), pred_gain_mlp.astype(F32))

    encoded, enc_kept = block_forward(value, enc_gains, enc_w, same, HEAD_DIM)
    enc_low = encoded.astype(BF)
    e = mm("td,cd->tc", enc_low, embed_all)
    start = jnp.where(masked, mask_token.astype(F32), e)
    predicted, pred_kept = block_forward(start, pred_gains, pred_w, same, P_HEAD_DIM)
    d_start, pred_g, pred_dg = block_backward(grad, pred_kept, pred_gains, pred_w, P_HEAD_DIM)
    d_token = jnp.sum(jnp.where(masked, d_start, 0.0), 0)
    d_e = jnp.where(masked, 0.0, d_start).astype(BF)
    d_e_rel = d_e.reshape(length, 4, -1)[:, jnp.arange(4) ^ me]
    g_embed = mm("td,tsc->sdc", enc_low, d_e_rel).astype(BF)
    d_enc = mm("tc,cd->td", d_e, embed_all)
    d_value, enc_g, enc_dg = block_backward(d_enc, enc_kept, enc_gains, enc_w, HEAD_DIM)

    r_pred = reduce_shards(jnp.concatenate(pred_g, -1))
    r_embed = reduce_shards(g_embed)
    r_down = reduce_shards(enc_g[2])
    r_up = reduce_shards(enc_g[1])
    r_attn = reduce_shards(enc_g[0])

    small = jnp.concatenate(
        [enc_dg[0], enc_dg[1], pred_dg[0], pred_dg[1], d_token, jnp.sum(predicted, 0), jnp.sum(predicted * predicted, 0)]
    )
    small = small.reshape(-1, 128)
    for axis in ("mp", "dp"):
        bit = 1
        while bit < lax.axis_size(axis):
            small = small + swap(small, axis, bit)
            bit *= 2
    small = small.reshape(-1)
    d_index = lax.axis_index("dp")

    def dp_slice(lo, n):
        return lax.dynamic_slice_in_dim(small[lo : lo + n], d_index * (n // dp_size), n // dp_size)

    c0 = 2 * width
    count = dp_size * patches.shape[0] * length
    mean = small[c0 + 3 * channels : c0 + 4 * channels] / count
    square = small[c0 + 4 * channels : c0 + 5 * channels] / count
    var_all = square - mean * mean
    n_var = channels // 4
    variance = lax.dynamic_slice_in_dim(var_all, me * n_var, n_var)

    predictions = spread_rows(predicted.astype(BF), me)
    patches_grad = spread_rows(d_value.astype(BF), me)

    def qkv_of(block, n):
        return jnp.stack([block[:, i * n : (i + 1) * n] for i in range(3)])

    return (
        predictions,
        patches_grad,
        variance,
        dp_slice(0, width),
        qkv_of(r_attn, hd),
        r_attn[:, 3 * hd :].T,
        dp_slice(width, width),
        r_up,
        r_down.T,
        r_embed,
        dp_slice(c0 + 2 * channels, channels),
        dp_slice(c0, channels),
        qkv_of(r_pred, p_hd),
        r_pred[:, 3 * p_hd : 4 * p_hd].T,
        dp_slice(c0 + channels, channels),
        r_pred[:, 4 * p_hd : 4 * p_hd + p_hid],
        r_pred[:, 4 * p_hd + p_hid :].T,
    )


def solution(mesh):
    placed = (
        P("dp", None, None), P("dp", None), P("dp", None), P(), P(None, None, "mp"), P("mp", None), P(),
        P(None, "mp"), P("mp", None), P(None, "mp"), P(), P(), P(None, None, "mp"), P("mp", None), P(),
        P(None, "mp"), P("mp", None), P("dp", None, None),
    )
    return jax.shard_map(
        body,
        mesh=mesh,
        in_specs=placed,
        out_specs=(
            P("dp", None, None), P("dp", None, None), P("mp"), P("dp"), P(None, "dp", "mp"), P("mp", "dp"),
            P("dp"), P("dp", "mp"), P("mp", "dp"), P("dp", "mp"), P("dp"), P("dp"), P(None, "dp", "mp"),
            P("mp", "dp"), P("dp"), P("dp", "mp"), P("mp", "dp"),
        ),
        check_vma=False,
    )
```

time: 1340 us -> 412 us (0.31)
  waiting for transfers between devices: 1060 us -> 161 us
  starting transfers between devices: 2.23 us -> 49.5 us
  blocking collectives: 37.4 us -> 0 us
  matrix products: 97.9 us -> 70.2 us
  between operations: 17.7 us -> 2.89 us
    reduce_scatter x15 -> x0, waiting for transfers between devices: 634 us -> none  [the longest x9 280 us: across_heads(): share = lax.psum_scatter(portion, 'mp', scatter_dimension=0, tiled=True)]
    all_gather x10 -> x0, waiting for transfers between devices: 243 us -> none  [the longest x9 224 us: across_heads(): return lax.all_gather(share, 'mp', axis=0, tiled=True)]
    unnamed x31 -> x0, waiting for transfers between devices: 183 us -> none
    ppermute x0 -> x34, waiting for transfers between devices: none -> 142 us  [swap(): return lax.ppermute(value, axis, [(i, i ^ bit) for i in range(size)])]
    psum x1 -> x0, blocking collectives: 37.4 us -> none  [body(): stat_sums = lax.psum((local_first, local_squares), 'dp')]
    dot_general x50 -> x49, matrix products: 94.1 us -> 62.8 us  [mm(): return jnp.einsum(spec, left, right, preferred_element_type=F32)]
    all_to_all x0 -> x5, starting transfers between devices: none -> 26.4 us  [reduce_shards(): lax.all_to_all(total, 'dp', 0, 0, tiled=True).reshape(size, rows, -1)]
    reduce_sum x20 -> x11, other arithmetic: 34.4 us -> 8.58 us  [the longest x5 6.78 us: reduce_shards(): return jnp.sum(parts.astype(F32), 0)]
  transfers between devices with their start and end apart: 28 -> 39, of which waited for: 28 -> 15; matrix products, arithmetic and copies ran while one was open for 6% -> 29% of each run, Pallas kernels for 0% -> 0%
where the time goes in v1:
time: 412 us; the launch traced here: 407 us
  waiting for transfers between devices  161 us (39%)
  matrix products  70.2 us (17%)
  local copies, waits for them, and re-layouts  68.9 us (17%)
  other arithmetic  54.6 us (13%)
  starting transfers between devices  49.5 us (12%)
    ppermute x34, waiting for transfers between devices, swap(): return lax.ppermute(value, axis, [(i, i ^ bit) for i in range(size)])  142 us
    dot_general x49, matrix products, mm(): return jnp.einsum(spec, left, right, preferred_element_type=F32)  62.8 us
    all_to_all x5, starting transfers between devices, reduce_shards(): lax.all_to_all(total, 'dp', 0, 0, tiled=True).reshape(size, rows, -1)  26.4 us
    unnamed x278, local copies, waits for them, and re-layouts  26.2 us
    ppermute x34, starting transfers between devices, swap(): return lax.ppermute(value, axis, [(i, i ^ bit) for i in range(size)])  23.1 us
    all_to_all x5, waiting for transfers between devices, reduce_shards(): lax.all_to_all(total, 'dp', 0, 0, tiled=True).reshape(size, rows, -1)  19.5 us
    convert_element_type x5, other arithmetic, reduce_shards(): total = (pair[0] + other.astype(F32)).astype(BF)  9.69 us
    add x5, other arithmetic, reduce_shards(): pair = jnp.stack([grads[0], grads[2]]).astype(F32) + away.astype(F32)  8.69 us
  transfers between devices with their start and end apart: 39, of which 15 were waited for; matrix products, arithmetic and copies ran while one was open for 29% of the time, Pallas kernels for 0%

profile of v1, /device:TPU:0, one launch (start us, length us, event | category | flops | bytes accessed | tf_op | source)
XLA Modules:
  0.0 407.5 jit_solution(8565095649186706697)
XLA Ops:
  1.2 2.6 collective-permute-start.10
  15.6 14.9 %collective-permute-done.13 = bf16[1152,384]{1,0:T(8,128)(2,1)} collective-permute-done((bf16[1152,384]{1,0:T(8,128)(2,1)}, bf16[1152,384]{1,0:T(8,128)(2,1)}, u32[]{:S(2)}, u32[]{:S(2)}) %collective-permute-start.13) | collective-permute-done | bytes 884768 | tf_op jit(solution)/shard_map/ppermute | solution.py:15
  37.7 18.1 %collective-permute-done.1 = bf16[768,768]{1,0:T(8,128)(2,1)} collective-permute-done((bf16[768,768]{1,0:T(8,128)(2,1)S(1)}, bf16[768,768]{1,0:T(8,128)(2,1)}, u32[]{:S(2)}, u32[]{:S(2)}) %collective-permute-start.1) | collective-permute-done | bytes 1179680 | tf_op jit(solution)/shard_map/ppermute | solution.py:15
  60.7 20.4 %collective-permute-done.7 = bf16[768,768]{1,0:T(8,128)(2,1)} collective-permute-done((bf16[768,768]{1,0:T(8,128)(2,1)}, bf16[768,768]{1,0:T(8,128)(2,1)}, u32[]{:S(2)}, u32[]{:S(2)}) %collective-permute-start.7) | collective-permute-done | bytes 1179680 | tf_op jit(solution)/shard_map/ppermute | solution.py:15
  83.4 22.1 %collective-permute-done.4 = bf16[768,768]{0,1:T(8,128)(2,1)} collective-permute-done((bf16[768,768]{0,1:T(8,128)(2,1)}, bf16[768,768]{0,1:T(8,128)(2,1)}, u32[]{:S(2)}, u32[]{:S(2)}) %collective-permute-start.4) | collective-permute-done | bytes 1179680 | tf_op jit(solution)/shard_map/ppermute | solution.py:15
  116.4 4.0 fusion.151
  122.6 2.4 constant_dynamic-update-slice_fusion
  127.5 7.0 %multiply_convert_fusion = (bf16[256,3072]{1,0:T(8,128)(2,1)S(1)}, f32[256,3072]{1,0:T(8,128)}) fusion(bf16[768,768]{0,1:T(8,128)(2,1)} %collective-permute-done.5, bf16[768,768]{0,1:T(8,128)(2,1)} %collective-permute-done.4, bf16[768,768]{0,1:T(8,128)(2,1)} %collective-permute-done.3, bf16[768,768]{0,1:T(8,128)(2,1)} %bitcast.18, ...), kind=kOutput, calls=%fused_computation.33 | convolution fusion | flops 1231552512 | bytes 10228736 | tf_op jit(solution)/shard_map/td,hd->th/dot_general | solution.py:23
  138.7 3.4 fusion.154
  147.7 4.7 %fusion.11 = bf16[256,1536]{1,0:T(8,128)(2,1)S(1)} fusion(f32[256,1536]{1,0:T(8,128)S(1)} %get-tuple-element.172, bf16[384,384]{1,0:T(8,128)(2,1)S(1)} %copy-done.88, bf16[384,384]{1,0:T(8,128)(2,1)S(1)} %copy-done.84, bf16[384,384]{1,0:T(8,128)(2,1)S(1)} %copy-done.86, bf16[384,384]{1,0:T(8,128)(2,1)S(1)} %copy-done.82, bf16[4,256,384]{2,1,0:T(8,128)(2,1)} %param.35, ...), kind=kOutput, calls=%fused_computation.39 | convolution fusion | flops 310640640 | bytes 3735556 | tf_op jit(solution)/shard_map/td,hd->th/dot_general | solution.py:23
  169.3 6.3 %fusion.2 = bf16[256,3072]{1,0:T(8,128)(2,1)S(1)} fusion(bf16[3072,768]{1,0:T(8,128)(2,1)} %constant_dynamic-update-slice_fusion, f32[256,3072]{1,0:T(8,128)} %get-tuple-element.164, f32[256,768]{1,0:T(8,128)S(1)} %fusion.157), kind=kOutput, calls=%fused_computation.20 | convolution fusion | flops 1216020480 | bytes 10223616 | tf_op jit(solution)/shard_map/td,hd->th/dot_general | solution.py:23
  175.7 5.0 %multiply_reduce_fusion = (f32[768]{0:T(1024)}, f32[256]{0:T(256)S(1)}, f32[256]{0:T(256)S(1)}, f32[256,768]{1,0:T(8,128)S(1)}) fusion(f32[256,768]{1,0:T(8,128)S(1)} %copy-done.5, f32[256]{0:T(256)S(1)} %copy-done.113, f32[256]{0:T(256)S(1)} %copy-done.106, f32[768]{0:T(1024)S(1)} %convert_element_type.334, bf16[256,3072]{1,0:T(8,128)(2,1)S(1)} %fusion.2, ...), kind=kOutput, calls=%fused_computation.174 | convolution fusion | flops 1228405504 | bytes 7874560 | tf_op jit(solution)/shard_map/th,hd->td/dot_general | solution.py:23
  224.8 5.8 %all-to-all-start.3 = ((bf16[8,96,96]{1,2,0:T(8,128)(2,1)}), bf16[8,96,96]{1,2,0:T(8,128)(2,1)S(1)}, u32[]{:S(2)}, u32[]{:S(2)}) async-start(bf16[8,96,96]{1,2,0:T(8,128)(2,1)} %copy.107), calls=%async_computation.3 | async-start | bytes 393216 | tf_op jit(solution)/shard_map/all_to_all | solution.py:113
  230.7 2.6 convert_add_fusion
  237.1 7.1 %collective-permute-done.33 = bf16[384,1152]{0,1:T(8,128)(2,1)} collective-permute-done((bf16[384,1152]{0,1:T(8,128)(2,1)}, bf16[384,1152]{0,1:T(8,128)(2,1)}, u32[]{:S(2)}, u32[]{:S(2)}) %collective-permute-start.33) | collective-permute-done | bytes 884768 | tf_op jit(solution)/shard_map/ppermute | solution.py:15
  246.5 2.4 copy.111
  249.6 6.5 %all-to-all-start.4 = ((bf16[8,48,1152]{2,1,0:T(8,128)(2,1)}), bf16[8,48,1152]{2,1,0:T(8,128)(2,1)}, u32[]{:S(2)}, u32[]{:S(2)}) async-start(bf16[8,48,1152]{2,1,0:T(8,128)(2,1)} %bitcast.365), calls=%async_computation.4 | async-start | bytes 1769472 | tf_op jit(solution)/shard_map/all_to_all | solution.py:113
  258.4 3.0 fusion.75
  262.1 6.3 %collective-permute-done.29 = bf16[768,768]{1,0:T(8,128)(2,1)} collective-permute-done((bf16[768,768]{1,0:T(8,128)(2,1)}, bf16[768,768]{1,0:T(8,128)(2,1)}, u32[]{:S(2)}, u32[]{:S(2)}) %collective-permute-start.29) | collective-permute-done | bytes 1179680 | tf_op jit(solution)/shard_map/ppermute | solution.py:15
  268.5 2.7 fusion.15
  271.2 5.6 %all-to-all-done.4 = bf16[8,48,1152]{2,1,0:T(8,128)(2,1)} async-done(((bf16[8,48,1152]{2,1,0:T(8,128)(2,1)}), bf16[8,48,1152]{2,1,0:T(8,128)(2,1)}, u32[]{:S(2)}, u32[]{:S(2)}) %all-to-all-start.4) | async-done | bytes 884768 | tf_op jit(solution)/shard_map/all_to_all | solution.py:113
  276.8 4.2 %all-to-all-start.2 = ((bf16[8,96,768]{2,1,0:T(8,128)(2,1)}), bf16[8,96,768]{2,1,0:T(8,128)(2,1)}, u32[]{:S(2)}, u32[]{:S(2)}) async-start(bf16[8,96,768]{2,1,0:T(8,128)(2,1)} %bitcast.360), calls=%async_computation.2 | async-start | bytes 2359296 | tf_op jit(solution)/shard_map/all_to_all | solution.py:113
  281.0 2.8 convert_add_fusion.2
  292.0 23.8 %collective-permute-done.20 = f32[27,128]{1,0:T(8,128)S(1)} collective-permute-done((f32[27,128]{1,0:T(8,128)S(1)}, f32[27,128]{1,0:T(8,128)S(1)}, u32[]{:S(2)}, u32[]{:S(2)}) %collective-permute-start.20) | collective-permute-done | bytes 13856 | tf_op jit(solution)/shard_map/ppermute | solution.py:15
  323.3 2.6 collective-permute-start.23
  326.0 3.2 fusion.19
  329.2 2.4 copy.101
  331.6 4.3 %all-to-all-start = ((bf16[8,96,768]{2,1,0:T(8,128)(2,1)}), bf16[8,96,768]{2,1,0:T(8,128)(2,1)}, u32[]{:S(2)}, u32[]{:S(2)}) async-start(bf16[8,96,768]{2,1,0:T(8,128)(2,1)} %bitcast.359), calls=%async_computation | async-start | bytes 2359296 | tf_op jit(solution)/shard_map/all_to_all | solution.py:113
  335.9 2.8 convert_add_fusion.1
  345.5 22.9 %collective-permute-done.17 = bf16[256,768]{1,0:T(8,128)(2,1)S(1)} collective-permute-done((bf16[256,768]{1,0:T(8,128)(2,1)S(1)}, bf16[256,768]{1,0:T(8,128)(2,1)S(1)}, u32[]{:S(2)}, u32[]{:S(2)}) %collective-permute-start.17) | collective-permute-done | bytes 393248 | tf_op jit(solution)/shard_map/ppermute | solution.py:15
  371.5 5.6 %all-to-all-start.1 = ((bf16[8,96,768]{2,1,0:T(8,128)(2,1)}), bf16[8,96,768]{2,1,0:T(8,128)(2,1)S(1)}, u32[]{:S(2)}, u32[]{:S(2)}) async-start(bf16[8,96,768]{2,1,0:T(8,128)(2,1)} %bitcast.80), calls=%async_computation.1 | async-start | bytes 2359296 | tf_op jit(solution)/shard_map/all_to_all | solution.py:113
  392.5 13.9 %all-to-all-done.1 = bf16[8,96,768]{2,1,0:T(8,128)(2,1)S(1)} async-done(((bf16[8,96,768]{2,1,0:T(8,128)(2,1)}), bf16[8,96,768]{2,1,0:T(8,128)(2,1)S(1)}, u32[]{:S(2)}, u32[]{:S(2)}) %all-to-all-start.1) | async-done | bytes 1179680 | tf_op jit(solution)/shard_map/all_to_all | solution.py:113
  (498 shorter events, 162.9 us)
Async XLA Ops:
  0.7 11.2 %collective-permute-start.9 = (bf16[96,768]{1,0:T(8,128)(2,1)}, bf16[96,768]{1,0:T(8,128)(2,1)S(1)}, u32[]{:S(2)}, u32[]{:S(2)}) collective-permute-start(bf16[96,768]{1,0:T(8,128)(2,1)} %bitcast.432), channel_id=1, source_target_pairs={{0,1},{1,0},{2,3},{3,2},{4,5},{5,4},{6,7},{7,6},{8,9},{9,8},{10,11... | collective-permute-start | bytes 442376 | tf_op jit(solution)/shard_map/ppermute | solution.py:15
  7.7 22.8 %collective-permute-start.13 = (bf16[1152,384]{1,0:T(8,128)(2,1)}, bf16[1152,384]{1,0:T(8,128)(2,1)}, u32[]{:S(2)}, u32[]{:S(2)}) collective-permute-start(bf16[1152,384]{1,0:T(8,128)(2,1)} %pad_maximum_fusion.12), channel_id=1, source_target_pairs={{0,2},{1,3},{2,0},{3,1},{4,6},{5,7},{6,4},{7,5},{8,10},{9,11},{10,... | collective-permute-start | bytes 2654216 | tf_op jit(solution)/shard_map/ppermute | solution.py:15
  7.7 24.2 %collective-permute-start.12 = (bf16[1152,384]{1,0:T(8,128)(2,1)}, bf16[1152,384]{1,0:T(8,128)(2,1)}, u32[]{:S(2)}, u32[]{:S(2)}) collective-permute-start(bf16[1152,384]{1,0:T(8,128)(2,1)} %pad_maximum_fusion.12), channel_id=1, source_target_pairs={{0,1},{1,0},{2,3},{3,2},{4,5},{5,4},{6,7},{7,6},{8,9},{9,8},{10,11... | collective-permute-start | bytes 2654216 | tf_op jit(solution)/shard_map/ppermute | solution.py:15
  8.0 47.8 %collective-permute-start.1 = (bf16[768,768]{1,0:T(8,128)(2,1)S(1)}, bf16[768,768]{1,0:T(8,128)(2,1)}, u32[]{:S(2)}, u32[]{:S(2)}) collective-permute-start(bf16[768,768]{1,0:T(8,128)(2,1)S(1)} %pad_maximum_fusion.8), channel_id=1, source_target_pairs={{0,2},{1,3},{2,0},{3,1},{4,6},{5,7},{6,4},{7,5},{8,10},{9,11},{10,... | collective-permute-start | bytes 3538952 | tf_op jit(solution)/shard_map/ppermute | solution.py:15
  11.9 44.0 %collective-permute-start.6 = (bf16[768,768]{1,0:T(8,128)(2,1)}, bf16[768,768]{1,0:T(8,128)(2,1)}, u32[]{:S(2)}, u32[]{:S(2)}) collective-permute-start(bf16[768,768]{1,0:T(8,128)(2,1)} %param.26), channel_id=1, source_target_pairs={{0,1},{1,0},{2,3},{3,2},{4,5},{5,4},{6,7},{7,6},{8,9},{9,8},{10,11... | collective-permute-start | bytes 3538952 | tf_op jit(solution)/shard_map/ppermute | solution.py:15
  15.1 66.0 %collective-permute-start.7 = (bf16[768,768]{1,0:T(8,128)(2,1)}, bf16[768,768]{1,0:T(8,128)(2,1)}, u32[]{:S(2)}, u32[]{:S(2)}) collective-permute-start(bf16[768,768]{1,0:T(8,128)(2,1)} %param.26), channel_id=1, source_target_pairs={{0,2},{1,3},{2,0},{3,1},{4,6},{5,7},{6,4},{7,5},{8,10},{9,11},{10,... | collective-permute-start | bytes 3538952 | tf_op jit(solution)/shard_map/ppermute | solution.py:15
  30.5 75.1 %collective-permute-start.4 = (bf16[768,768]{0,1:T(8,128)(2,1)}, bf16[768,768]{0,1:T(8,128)(2,1)}, u32[]{:S(2)}, u32[]{:S(2)}) collective-permute-start(bf16[768,768]{0,1:T(8,128)(2,1)} %bitcast.18), channel_id=1, source_target_pairs={{0,2},{1,3},{2,0},{3,1},{4,6},{5,7},{6,4},{7,5},{8,10},{9,11},{10,... | collective-permute-start | bytes 3538952 | tf_op jit(solution)/shard_map/ppermute | solution.py:15
  31.9 73.7 %collective-permute-start.14 = (bf16[1152,384]{1,0:T(8,128)(2,1)}, bf16[1152,384]{1,0:T(8,128)(2,1)}, u32[]{:S(2)}, u32[]{:S(2)}) collective-permute-start(bf16[1152,384]{1,0:T(8,128)(2,1)} %collective-permute-done.13), channel_id=1, source_target_pairs={{0,1},{1,0},{2,3},{3,2},{4,5},{5,4},{6,7},{7,6},{8,9},{9,8},{10,11... | collective-permute-start | bytes 2654216 | tf_op jit(solution)/shard_map/ppermute | solution.py:15
  55.8 53.6 %collective-permute-start = (bf16[768,768]{1,0:T(8,128)(2,1)S(1)}, bf16[768,768]{1,0:T(8,128)(2,1)S(1)}, u32[]{:S(2)}, u32[]{:S(2)}) collective-permute-start(bf16[768,768]{1,0:T(8,128)(2,1)S(1)} %pad_maximum_fusion.8), channel_id=1, source_target_pairs={{0,1},{1,0},{2,3},{3,2},{4,5},{5,4},{6,7},{7,6},{8,9},{9,8},{10,11... | collective-permute-start | bytes 3538952 | tf_op jit(solution)/shard_map/ppermute | solution.py:15
  55.8 53.6 %collective-permute-start.2 = (bf16[768,768]{1,0:T(8,128)(2,1)}, bf16[768,768]{1,0:T(8,128)(2,1)S(1)}, u32[]{:S(2)}, u32[]{:S(2)}) collective-permute-start(bf16[768,768]{1,0:T(8,128)(2,1)} %collective-permute-done.1), channel_id=1, source_target_pairs={{0,1},{1,0},{2,3},{3,2},{4,5},{5,4},{6,7},{7,6},{8,9},{9,8},{10,11... | collective-permute-start | bytes 3538952 | tf_op jit(solution)/shard_map/ppermute | solution.py:15
  81.1 46.4 %collective-permute-start.3 = (bf16[768,768]{0,1:T(8,128)(2,1)}, bf16[768,768]{0,1:T(8,128)(2,1)}, u32[]{:S(2)}, u32[]{:S(2)}) collective-permute-start(bf16[768,768]{0,1:T(8,128)(2,1)} %bitcast.18), channel_id=1, source_target_pairs={{0,1},{1,0},{2,3},{3,2},{4,5},{5,4},{6,7},{7,6},{8,9},{9,8},{10,11... | collective-permute-start | bytes 3538952 | tf_op jit(solution)/shard_map/ppermute | solution.py:15
  105.6 17.0 %collective-permute-start.8 = (bf16[768,768]{1,0:T(8,128)(2,1)}, bf16[768,768]{1,0:T(8,128)(2,1)}, u32[]{:S(2)}, u32[]{:S(2)}) collective-permute-start(bf16[768,768]{1,0:T(8,128)(2,1)} %collective-permute-done.7), channel_id=1, source_target_pairs={{0,1},{1,0},{2,3},{3,2},{4,5},{5,4},{6,7},{7,6},{8,9},{9,8},{10,11... | collective-permute-start | bytes 3538952 | tf_op jit(solution)/shard_map/ppermute | solution.py:15
  105.6 21.9 %collective-permute-start.5 = (bf16[768,768]{0,1:T(8,128)(2,1)}, bf16[768,768]{0,1:T(8,128)(2,1)}, u32[]{:S(2)}, u32[]{:S(2)}) collective-permute-start(bf16[768,768]{0,1:T(8,128)(2,1)} %collective-permute-done.4), channel_id=1, source_target_pairs={{0,1},{1,0},{2,3},{3,2},{4,5},{5,4},{6,7},{7,6},{8,9},{9,8},{10,11... | collective-permute-start | bytes 3538952 | tf_op jit(solution)/shard_map/ppermute | solution.py:15
  192.8 24.9 %collective-permute-start.30 = (bf16[2,768,96]{1,2,0:T(8,128)(2,1)S(1)}, bf16[2,768,96]{1,2,0:T(8,128)(2,1)S(1)}, u32[]{:S(2)}, u32[]{:S(2)}) collective-permute-start(bf16[2,768,96]{1,2,0:T(8,128)(2,1)S(1)} %pad_maximum_fusion.21), channel_id=1, source_target_pairs={{0,1},{1,0},{2,3},{3,2},{4,5},{5,4},{6,7},{7,6},{8,9},{9,8},{10,11... | collective-permute-start | bytes 884744 | tf_op jit(solution)/shard_map/ppermute | solution.py:15
  204.0 26.6 %collective-permute-start.28 = (bf16[2,768,768]{2,1,0:T(8,128)(2,1)}, bf16[2,768,768]{2,1,0:T(8,128)(2,1)}, u32[]{:S(2)}, u32[]{:S(2)}) collective-permute-start(bf16[2,768,768]{2,1,0:T(8,128)(2,1)} %pad_maximum_fusion.5), channel_id=1, source_target_pairs={{0,1},{1,0},{2,3},{3,2},{4,5},{5,4},{6,7},{7,6},{8,9},{9,8},{10,11... | collective-permute-start | bytes 7077896 | tf_op jit(solution)/shard_map/ppermute | solution.py:15
  210.6 70.4 %collective-permute-start.24 = (bf16[2,768,768]{1,2,0:T(8,128)(2,1)}, bf16[2,768,768]{1,2,0:T(8,128)(2,1)}, u32[]{:S(2)}, u32[]{:S(2)}) collective-permute-start(bf16[2,768,768]{1,2,0:T(8,128)(2,1)} %pad_maximum_fusion.3), channel_id=1, source_target_pairs={{0,1},{1,0},{2,3},{3,2},{4,5},{5,4},{6,7},{7,6},{8,9},{9,8},{10,11... | collective-permute-start | bytes 7077896 | tf_op jit(solution)/shard_map/ppermute | solution.py:15
  216.0 119.9 %collective-permute-start.26 = (bf16[2,768,768]{2,1,0:T(8,128)(2,1)}, bf16[2,768,768]{2,1,0:T(8,128)(2,1)}, u32[]{:S(2)}, u32[]{:S(2)}) collective-permute-start(bf16[2,768,768]{2,1,0:T(8,128)(2,1)} %pad_maximum_fusion.4), channel_id=1, source_target_pairs={{0,1},{1,0},{2,3},{3,2},{4,5},{5,4},{6,7},{7,6},{8,9},{9,8},{10,11... | collective-permute-start | bytes 7077896 | tf_op jit(solution)/shard_map/ppermute | solution.py:15
  221.4 22.8 %collective-permute-start.33 = (bf16[384,1152]{0,1:T(8,128)(2,1)}, bf16[384,1152]{0,1:T(8,128)(2,1)}, u32[]{:S(2)}, u32[]{:S(2)}) collective-permute-start(bf16[384,1152]{0,1:T(8,128)(2,1)} %fusion.67), channel_id=1, source_target_pairs={{0,2},{1,3},{2,0},{3,1},{4,6},{5,7},{6,4},{7,5},{8,10},{9,11},{10,... | collective-permute-start | bytes 2654216 | tf_op jit(solution)/shard_map/ppermute | solution.py:15
  224.8 24.1 %all-to-all-start.3 = ((bf16[8,96,96]{1,2,0:T(8,128)(2,1)}), bf16[8,96,96]{1,2,0:T(8,128)(2,1)S(1)}, u32[]{:S(2)}, u32[]{:S(2)}) async-start(bf16[8,96,96]{1,2,0:T(8,128)(2,1)} %copy.107), calls=%async_computation.3 | async-start | bytes 393216 | tf_op jit(solution)/shard_map/all_to_all | solution.py:113
  236.6 31.9 %collective-permute-start.29 = (bf16[768,768]{1,0:T(8,128)(2,1)}, bf16[768,768]{1,0:T(8,128)(2,1)}, u32[]{:S(2)}, u32[]{:S(2)}) collective-permute-start(bf16[768,768]{1,0:T(8,128)(2,1)} %fusion.50), channel_id=1, source_target_pairs={{0,2},{1,3},{2,0},{3,1},{4,6},{5,7},{6,4},{7,5},{8,10},{9,11},{10,... | collective-permute-start | bytes 3538952 | tf_op jit(solution)/shard_map/ppermute | solution.py:15
  249.6 27.1 %all-to-all-start.4 = ((bf16[8,48,1152]{2,1,0:T(8,128)(2,1)}), bf16[8,48,1152]{2,1,0:T(8,128)(2,1)}, u32[]{:S(2)}, u32[]{:S(2)}) async-start(bf16[8,48,1152]{2,1,0:T(8,128)(2,1)} %bitcast.365), calls=%async_computation.4 | async-start | bytes 1769472 | tf_op jit(solution)/shard_map/all_to_all | solution.py:113
  276.8 54.8 %all-to-all-start.2 = ((bf16[8,96,768]{2,1,0:T(8,128)(2,1)}), bf16[8,96,768]{2,1,0:T(8,128)(2,1)}, u32[]{:S(2)}, u32[]{:S(2)}) async-start(bf16[8,96,768]{2,1,0:T(8,128)(2,1)} %bitcast.360), calls=%async_computation.2 | async-start | bytes 2359296 | tf_op jit(solution)/shard_map/all_to_all | solution.py:113
  287.2 38.8 %collective-permute-start.25 = (bf16[768,768]{0,1:T(8,128)(2,1)}, bf16[768,768]{0,1:T(8,128)(2,1)}, u32[]{:S(2)}, u32[]{:S(2)}) collective-permute-start(bf16[768,768]{0,1:T(8,128)(2,1)} %fusion.48), channel_id=1, source_target_pairs={{0,2},{1,3},{2,0},{3,1},{4,6},{5,7},{6,4},{7,5},{8,10},{9,11},{10,... | collective-permute-start | bytes 3538952 | tf_op jit(solution)/shard_map/ppermute | solution.py:15
  290.0 25.8 %collective-permute-start.20 = (f32[27,128]{1,0:T(8,128)S(1)}, f32[27,128]{1,0:T(8,128)S(1)}, u32[]{:S(2)}, u32[]{:S(2)}) collective-permute-start(f32[27,128]{1,0:T(8,128)S(1)} %bitcast_add_fusion), channel_id=1, source_target_pairs={{0,2},{1,3},{2,0},{3,1},{4,6},{5,7},{6,4},{7,5},{8,10},{9,11},{10,... | collective-permute-start | bytes 41480 | tf_op jit(solution)/shard_map/ppermute | solution.py:15
  290.5 51.3 %collective-permute-start.15 = (bf16[256,384]{1,0:T(8,128)(2,1)S(1)}, bf16[256,384]{1,0:T(8,128)(2,1)S(1)}, u32[]{:S(2)}, u32[]{:S(2)}) collective-permute-start(bf16[256,384]{1,0:T(8,128)(2,1)S(1)} %get-tuple-element.140), channel_id=1, source_target_pairs={{0,2},{1,3},{2,0},{3,1},{4,6},{5,7},{6,4},{7,5},{8,10},{9,11},{10,... | collective-permute-start | bytes 589832 | tf_op jit(solution)/shard_map/ppermute | solution.py:15
  323.3 18.5 %collective-permute-start.23 = (f32[27,128]{1,0:T(8,128)S(1)}, f32[27,128]{1,0:T(8,128)S(1)}, u32[]{:S(2)}, u32[]{:S(2)}) collective-permute-start(f32[27,128]{1,0:T(8,128)S(1)} %add.193), channel_id=1, source_target_pairs={{0,16},{4,20},{8,24},{12,28},{16,0},{20,4},{24,8},{28,12},{1,17},{... | collective-permute-start | bytes 41480 | tf_op jit(solution)/shard_map/ppermute | solution.py:15
  331.6 39.9 %all-to-all-start = ((bf16[8,96,768]{2,1,0:T(8,128)(2,1)}), bf16[8,96,768]{2,1,0:T(8,128)(2,1)}, u32[]{:S(2)}, u32[]{:S(2)}) async-start(bf16[8,96,768]{2,1,0:T(8,128)(2,1)} %bitcast.359), calls=%async_computation | async-start | bytes 2359296 | tf_op jit(solution)/shard_map/all_to_all | solution.py:113
  338.9 31.2 %collective-permute-start.27 = (bf16[768,768]{1,0:T(8,128)(2,1)S(1)}, bf16[768,768]{1,0:T(8,128)(2,1)S(1)}, u32[]{:S(2)}, u32[]{:S(2)}) collective-permute-start(bf16[768,768]{1,0:T(8,128)(2,1)S(1)} %fusion.49), channel_id=1, source_target_pairs={{0,2},{1,3},{2,0},{3,1},{4,6},{5,7},{6,4},{7,5},{8,10},{9,11},{10,... | collective-permute-start | bytes 3538952 | tf_op jit(solution)/shard_map/ppermute | solution.py:15
  340.8 27.6 %collective-permute-start.17 = (bf16[256,768]{1,0:T(8,128)(2,1)S(1)}, bf16[256,768]{1,0:T(8,128)(2,1)S(1)}, u32[]{:S(2)}, u32[]{:S(2)}) collective-permute-start(bf16[256,768]{1,0:T(8,128)(2,1)S(1)} %fusion.74), channel_id=1, source_target_pairs={{0,2},{1,3},{2,0},{3,1},{4,6},{5,7},{6,4},{7,5},{8,10},{9,11},{10,... | collective-permute-start | bytes 1179656 | tf_op jit(solution)/shard_map/ppermute | solution.py:15
  341.9 27.5 %collective-permute-start.16 = (bf16[2,256,384]{2,1,0:T(8,128)(2,1)S(1)}, bf16[2,256,384]{2,1,0:T(8,128)(2,1)S(1)}, u32[]{:S(2)}, u32[]{:S(2)}) collective-permute-start(bf16[2,256,384]{2,1,0:T(8,128)(2,1)S(1)} %pad_maximum_fusion.18), channel_id=1, source_target_pairs={{0,1},{1,0},{2,3},{3,2},{4,5},{5,4},{6,7},{7,6},{8,9},{9,8},{10,11... | collective-permute-start | bytes 1179656 | tf_op jit(solution)/shard_map/ppermute | solution.py:15
  369.3 12.5 %collective-permute-start.18 = (bf16[2,256,768]{2,1,0:T(8,128)(2,1)}, bf16[2,256,768]{2,1,0:T(8,128)(2,1)S(1)}, u32[]{:S(2)}, u32[]{:S(2)}) collective-permute-start(bf16[2,256,768]{2,1,0:T(8,128)(2,1)} %pad_maximum_fusion.16), channel_id=1, source_target_pairs={{0,1},{1,0},{2,3},{3,2},{4,5},{5,4},{6,7},{7,6},{8,9},{9,8},{10,11... | collective-permute-start | bytes 2359304 | tf_op jit(solution)/shard_map/ppermute | solution.py:15
  371.5 34.9 %all-to-all-start.1 = ((bf16[8,96,768]{2,1,0:T(8,128)(2,1)}), bf16[8,96,768]{2,1,0:T(8,128)(2,1)S(1)}, u32[]{:S(2)}, u32[]{:S(2)}) async-start(bf16[8,96,768]{2,1,0:T(8,128)(2,1)} %bitcast.80), calls=%async_computation.1 | async-start | bytes 2359296 | tf_op jit(solution)/shard_map/all_to_all | solution.py:113
  (140 other events, 1098.2 us)
